TPU v7x, 128 devices: a whole 4x4x4 slice. The times are simulated.
128 devices in a mesh: grp: 8 (over x, z_hi), rsp: 16 (over y, z_lo, core).
Axes of the slice: x: 4, y: 4, z: 4 (z_hi: 2, z_lo: 2; z = z_hi * 2 + z_lo), core: 2. Of those that a mesh axis runs over, the one named last changes fastest.
Arguments:
- prompt_x: bfloat16 [8192, 5120], P(('grp', 'rsp')), may hold values from -6 to 6
- key_value_weight: bfloat16 [5120, 1024], replicated, may hold values from -0.078125 to 0.078125
- queries: bfloat16 [32768, 4096], P(('grp', 'rsp')), may hold values from -90 to 90
- resp_kv: bfloat16 [32768, 1024], P(('grp', 'rsp')), may hold values from -6 to 6
- out_grad: bfloat16 [32768, 4096], P(('grp', 'rsp')), may hold values from -6 to 6
- lengths: int32 [256], P(('grp', 'rsp')), may hold values from 1 to 128, 24576 in all
- token_mask: int32 [256, 128], P(('grp', 'rsp')), may hold values 0 or 1
Outputs:
- query_grad: bfloat16 [32768, 4096], P(('grp', 'rsp'))
- resp_kv_grad: bfloat16 [32768, 1024], P(('grp', 'rsp'))
- prompt_x_grad: bfloat16 [8192, 5120], P(('grp', 'rsp'))
- w_kv_grad: float32 [5120, 1024], P('rsp')
Inputs may be any that keep to these rules, and one draw needn't show every extreme that they name: `lengths`: between 1 and 128, the largest exactly 128.
All inputs are finite; a program needn't handle non-finite values. No bound on the sum of `lengths` or of `token_mask` on one device may be relied on, other than what follows from the above.
Results may differ from a plain program's by a relative error of at most 0.008.
Values may be sent and summed in bfloat16 or wider, within the bound.
A program may use at most 192 MiB of HBM per device.

v0:
```python
import functools

import jax
import jax.numpy as jnp
from jax import lax
from jax.experimental import pallas as pl
from jax.experimental.pallas import tpu as pltpu
from jax.sharding import PartitionSpec as P

HEADS = 4
PER = 8
D = 128
SEQ = 128
ROWS = PER * SEQ
PROMPT = 1024
KEYS = PROMPT + SEQ
TOK = 64
WIDTH = 5120
PEERS = 8
WROWS = 320
NX = 4
WPART = WROWS // NX
BF = jnp.bfloat16
F32 = jnp.float32
SCALE = D**-0.5
LOG2E = 1.4426950408889634
MESH = pl.DeviceIdType.MESH
NN = ((1,), (0,))
NT = ((1,), (1,))
TN = ((0,), (0,))


def dot(a, b, dims):
    return lax.dot_general(a, b, (dims, ((), ())), preferred_element_type=F32)


def lanes(start, size=D):
    return pl.ds(pl.multiple_of(start, D), size)


def kernel(
    x_hbm, w_hbm, q_hbm, kv_hbm, d_hbm, len_ref, mask_ref,
    qg, own_g, xg, wg,
    x, w, q, d, own,
    kv, pb, pr, rss, rsr, ga, xs, xr, ws, wr, zs, zr, wa,
    e0, s0, e1, s1, qd, r0, r1, xacc,
    in_sem, w_sem,
    kv_s, kv_r, kvp_s, kvp_r, p_s, p_r, rs_s, rs_r, ga_s, ga_r, gp_s, gp_r,
    x_s, x_r, w_s, w_r, z_s, z_r, wa_s, wa_r,
):
    g, r = lax.axis_index("grp"), lax.axis_index("rsp")
    core, at = r % 2, r // 2
    mate = at * 2 + 1 - core
    gx, gz = g // 2, g % 2
    z_mate = gx * 2 + 1 - gz
    mine = core * PEERS + at

    def remote(src, dst, send, recv, grp, rsp):
        return pltpu.make_async_remote_copy(
            src_ref=src, dst_ref=dst, send_sem=send, recv_sem=recv,
            device_id=(grp, rsp), device_id_type=MESH,
        )

    def each(count, f):
        def body(j, c):
            f(j)
            return c

        lax.fori_loop(1, count, body, 0)

    loads = [
        pltpu.make_async_copy(src, dst, in_sem.at[n])
        for n, (src, dst) in enumerate(((x_hbm, x), (q_hbm, q), (d_hbm, d), (kv_hbm, own)))
    ]

    def w_loads(h):
        return [
            pltpu.make_async_copy(
                w_hbm.at[:, pl.ds(t * 512 + h * D, D)], w.at[h, :, pl.ds(t * D, D)], w_sem.at[h, t]
            )
            for t in range(2)
        ]

    loads[0].start()
    for h in range(HEADS):
        for c in w_loads(h):
            c.start()
    for c in loads[1:]:
        c.start()

    barrier = pltpu.get_barrier_semaphore()
    each(16, lambda j: pl.semaphore_signal(
        barrier, inc=1, device_id=(g, (r + j) % 16), device_id_type=MESH))
    each(NX, lambda j: pl.semaphore_signal(
        barrier, inc=1, device_id=(((gx + j) % NX) * 2 + gz, r), device_id_type=MESH))
    pl.semaphore_signal(barrier, inc=1, device_id=(z_mate, r), device_id_type=MESH)

    def kv_copy(h, j, there):
        to = (at + j) % PEERS
        slot = core * PEERS + (to if there else at)
        return remote(kv.at[h, slot], kv.at[h, slot], kv_s.at[h, j],
                      kv_r.at[h, to if there else at], g, to * 2 + core)

    def kv_mate(h):
        half = kv.at[h, pl.ds(core * PEERS, PEERS)]
        return remote(half, half, kvp_s.at[h], kvp_r.at[h], g, mate)

    def kv_mate_in(h):
        half = kv.at[h, pl.ds((1 - core) * PEERS, PEERS)]
        return remote(half, half, kvp_s.at[h], kvp_r.at[h], g, mate)

    def p_copy(h):
        return remote(pb.at[h, pl.ds((1 - core) * PEERS, PEERS)], pr.at[h], p_s.at[h], p_r.at[h], g, mate)

    def rs_copy(h, j):
        to = (at + j) % PEERS
        return remote(rss.at[h, to], rsr.at[h, at], rs_s.at[h, j], rs_r.at[h, at], g, to * 2 + core)

    def rs_in(h, j):
        to = (at + j) % PEERS
        return remote(rss.at[h, to], rsr.at[h, to], rs_s.at[h, j], rs_r.at[h, to], g, to * 2 + core)

    def ga_copy(h, j, there):
        to = (at + j) % PEERS
        slot = core * PEERS + (to if there else at)
        return remote(ga.at[h, slot], ga.at[h, slot], ga_s.at[h, j],
                      ga_r.at[h, to if there else at], g, to * 2 + core)

    def ga_mate(h, side):
        half = ga.at[h, pl.ds(side * PEERS, PEERS)]
        return remote(half, half, gp_s.at[h], gp_r.at[h], g, mate)

    def x_copy(j):
        to = (r + j) % 16
        return remote(xs.at[to], xr.at[mine], x_s.at[j], x_r.at[mine], g, to)

    def x_in(j):
        to = (r + j) % 16
        slot = (to % 2) * PEERS + to // 2
        return remote(xs.at[to], xr.at[slot], x_s.at[j], x_r.at[slot], g, to)

    def w_copy(h, j):
        to = (gx + j) % NX
        return remote(ws.at[h, to], wr.at[h, gx], w_s.at[h, j], w_r.at[h, gx], to * 2 + gz, r)

    def w_in(h, j):
        to = (gx + j) % NX
        return remote(ws.at[h, to], wr.at[h, to], w_s.at[h, j], w_r.at[h, to], to * 2 + gz, r)

    def z_copy(h):
        return remote(zs.at[h], zr.at[h], z_s.at[h], z_r.at[h], z_mate, r)

    def wa_copy(h, j, there):
        to = (gx + j) % NX
        slot = to if there else gx
        return remote(wa.at[h, slot], wa.at[h, slot], wa_s.at[h, j], wa_r.at[h, slot], to * 2 + gz, r)

    loads[0].wait()
    for h in range(HEADS):
        for c in w_loads(h):
            c.wait()
        kv[h, mine] = dot(x[...], w[h], NN).astype(BF)
        if h == 0:
            pl.semaphore_wait(barrier, 15 + NX)
        each(PEERS, lambda j, h=h: kv_copy(h, j, False).start())
    for to in range(16):
        xs[to] = x[:, to * WROWS:(to + 1) * WROWS]
    xr[mine] = xs[r]

    for c in loads[1:]:
        c.wait()
    row = lax.broadcasted_iota(jnp.int32, (SEQ, D), 0)
    for n in range(2):
        live = jnp.broadcast_to(mask_ref[n:n + 1, :].astype(F32), (SEQ, SEQ)).T
        live = (live == 1.0) & (row < len_ref[n])
        rows = slice(n * SEQ, (n + 1) * SEQ)

        def clear(c, _, rows=rows, live=live):
            cols = lanes(c * D)
            d[rows, cols] = jnp.where(live, d[rows, cols].astype(F32), 0.0).astype(BF)
            return _

        lax.fori_loop(0, HEADS * PER, clear, 0)

    def kv_relay(h):
        each(PEERS, lambda j: kv_copy(h, j, True).wait_recv())
        kv_mate(h).start()

    kv_relay(0)
    each(16, lambda j: x_copy(j).start())

    es, ss, rr = (e0, e1), (s0, s1), (r0, r1)
    causal = (lax.broadcasted_iota(jnp.int32, (ROWS, SEQ), 1)
              <= lax.broadcasted_iota(jnp.int32, (ROWS, SEQ), 0) % SEQ)

    def own_kv(h, n):
        rows = slice(n * SEQ, (n + 1) * SEQ)
        return own[rows, lanes(h * D)], own[rows, lanes(512 + h * D)]

    def softmax_part(h, n):
        rows = slice(n * SEQ, (n + 1) * SEQ)
        qn = jnp.concatenate([q[rows, lanes((h * PER + t) * D)] for t in range(PER)], 0)
        dn = jnp.concatenate([d[rows, lanes((h * PER + t) * D)] for t in range(PER)], 0)
        keys = kv[h, :, :, 0:D].reshape(PROMPT, D)
        values = kv[h, :, :, D:].reshape(PROMPT, D)
        ko, vo = own_kv(h, n)
        none = jnp.zeros_like(ko)
        both = jnp.concatenate(
            [jnp.concatenate([ko, none], 1), jnp.concatenate([none, vo], 1)], 0)
        last = dot(jnp.concatenate([qn, dn], 1), both, NT)
        scores = jnp.concatenate(
            [dot(qn, keys, NT), jnp.where(causal, last[:, :SEQ], -1e30)], 1)
        pgrad = jnp.concatenate([dot(dn, values, NT), last[:, SEQ:]], 1)
        top = jnp.max(scores, axis=1, keepdims=True)
        e = jnp.exp2((scores - top) * (SCALE * LOG2E))
        inv = 1.0 / jnp.sum(e, axis=1, keepdims=True)
        center = jnp.sum(e * pgrad, axis=1, keepdims=True) * inv
        es[n][...] = e.astype(BF)
        ss[n][...] = (e * (pgrad - center)).astype(BF)
        rr[n][...] = jnp.broadcast_to(inv, (ROWS, D))
        qd[n, :, 0:D] = (qn * inv).astype(BF)
        qd[n, :, D:] = (dn * inv).astype(BF)

    def key_part(h):
        total = []
        for n in range(2):
            dk = dot(qd[n, :, 0:D], ss[n][...], TN) * SCALE
            dv = dot(qd[n, :, D:], es[n][...], TN)
            rows = slice(n * SEQ, (n + 1) * SEQ)
            own_g[rows, lanes(h * D)] = dk[:, PROMPT:].astype(BF).T
            own_g[rows, lanes(512 + h * D)] = dv[:, PROMPT:].astype(BF).T
            total.append((dk[:, :PROMPT], dv[:, :PROMPT]))
        dk, dv = total[0][0] + total[1][0], total[0][1] + total[1][1]
        pb[h, :, :, 0:D] = dk.astype(BF).T.reshape(16, TOK, D)
        pb[h, :, :, D:] = dv.astype(BF).T.reshape(16, TOK, D)

    def query_part(h, n):
        rows = slice(n * SEQ, (n + 1) * SEQ)
        keys = jnp.concatenate([kv[h, :, :, 0:D].reshape(PROMPT, D), own_kv(h, n)[0]], 0)
        out = (dot(ss[n][...], keys, NN) * (rr[n][...] * SCALE)).astype(BF)
        for t in range(PER):
            qg[rows, lanes((h * PER + t) * D)] = out[t * SEQ:(t + 1) * SEQ]

    def pair_sum(h):
        p_copy(h).wait_recv()
        half = pb[h, pl.ds(core * PEERS, PEERS)].astype(F32) + pr[h].astype(F32)
        rss[h] = half.astype(BF)
        rsr[h, at] = rss[h, at]
        each(PEERS, lambda j: rs_copy(h, j).start())

    def group_sum(h):
        each(PEERS, lambda j: rs_in(h, j).wait_recv())
        total = rsr[h, 0].astype(F32)
        for j in range(1, PEERS):
            total += rsr[h, j].astype(F32)
        ga[h, mine] = total.astype(BF)
        each(PEERS, lambda j: ga_copy(h, j, False).start())

    def spread(h):
        each(PEERS, lambda j: ga_copy(h, j, True).wait_recv())
        ga_mate(h, core).start()

    def x_part(h):
        def tile(c, _):
            rows = pl.ds(c * 1024, 1024)
            xacc[:, lanes(c * 1024, 1024)] += dot(ga[h, mine], w[h, rows, :], NT)
            return _

        lax.fori_loop(0, WIDTH // 1024, tile, 0)

    def w_part(h):
        ga_mate(h, 1 - core).wait_recv()
        part = dot(xr[...].reshape(PROMPT, WROWS), ga[h].reshape(PROMPT, 2 * D), TN)
        ws[h] = part.astype(BF).reshape(NX, WPART, 2 * D)
        wr[h, gx] = ws[h, gx]
        each(NX, lambda j: w_copy(h, j).start())

    def w_sum(h):
        each(NX, lambda j: w_in(h, j).wait_recv())
        total = wr[h, 0].astype(F32)
        for j in range(1, NX):
            total += wr[h, j].astype(F32)
        zs[h] = total.astype(BF)
        z_copy(h).start()

    def z_sum(h):
        z_copy(h).wait_recv()
        wa[h, gx] = (zs[h].astype(F32) + zr[h].astype(F32)).astype(BF)
        each(NX, lambda j: wa_copy(h, j, False).start())

    def w_out(h):
        each(NX, lambda j: wa_copy(h, j, True).wait_recv())
        full = wa[h].astype(F32).reshape(WROWS, 2 * D)
        wg[:, lanes(h * D)] = full[:, :D]
        wg[:, lanes(512 + h * D)] = full[:, D:]

    xacc[...] = jnp.zeros_like(xacc)

    def head(h, c):
        kv_mate_in(h).wait_recv()
        softmax_part(h, 0)

        @pl.when(h >= 1)
        def _():
            group_sum(h - 1)

        @pl.when(h >= 2)
        def _():
            w_sum(h - 2)

        @pl.when(h < HEADS - 1)
        def _():
            kv_relay(h + 1)

        softmax_part(h, 1)

        @pl.when(h == 0)
        def _():
            each(16, lambda j: x_in(j).wait_recv())

        @pl.when(h >= 1)
        def _():
            spread(h - 1)

        @pl.when(h >= 2)
        def _():
            z_sum(h - 2)

        key_part(h)
        p_copy(h).start()

        @pl.when(h >= 1)
        def _():
            x_part(h - 1)
            w_part(h - 1)

        pair_sum(h)
        query_part(h, 0)
        query_part(h, 1)

        @pl.when(h >= 2)
        def _():
            w_out(h - 2)

        return c

    lax.fori_loop(0, HEADS, head, 0)

    last = HEADS - 1
    w_sum(last - 1)
    group_sum(last)
    z_sum(last - 1)
    x_part(last)
    spread(last)
    xg[...] = xacc[...].astype(BF)
    w_out(last - 1)
    w_part(last)
    w_sum(last)
    z_sum(last)

    def sent(h, c):
        each(PEERS, lambda j: kv_copy(h, j, False).wait_send())
        kv_mate(h).wait_send()
        p_copy(h).wait_send()
        each(PEERS, lambda j: rs_copy(h, j).wait_send())
        each(PEERS, lambda j: ga_copy(h, j, False).wait_send())
        ga_mate(h, core).wait_send()
        each(NX, lambda j: w_copy(h, j).wait_send())
        z_copy(h).wait_send()
        each(NX, lambda j: wa_copy(h, j, False).wait_send())
        return c

    w_out(last)
    lax.fori_loop(0, HEADS, sent, 0)
    each(16, lambda j: x_copy(j).wait_send())


def local(prompt_x, key_value_weight, queries, resp_kv, out_grad, lengths, token_mask):
    dma = pltpu.SemaphoreType.DMA
    vmem = pl.BlockSpec(memory_space=pltpu.VMEM)
    hbm = pl.BlockSpec(memory_space=pl.ANY)
    pairs = lambda *shape: [dma(shape), dma(shape)]
    return pl.pallas_call(
        kernel,
        out_shape=(
            jax.ShapeDtypeStruct((2 * SEQ, HEADS * PER * D), BF),
            jax.ShapeDtypeStruct((2 * SEQ, 2 * HEADS * D), BF),
            jax.ShapeDtypeStruct((TOK, WIDTH), BF),
            jax.ShapeDtypeStruct((WROWS, 2 * HEADS * D), F32),
        ),
        in_specs=[hbm] * 5 + [pl.BlockSpec(memory_space=pltpu.SMEM), vmem],
        out_specs=(vmem,) * 4,
        scratch_shapes=[
            pltpu.VMEM((TOK, WIDTH), BF),
            pltpu.VMEM((HEADS, WIDTH, 2 * D), BF),
            pltpu.VMEM((2 * SEQ, HEADS * PER * D), BF),
            pltpu.VMEM((2 * SEQ, HEADS * PER * D), BF),
            pltpu.VMEM((2 * SEQ, 2 * HEADS * D), BF),
            pltpu.VMEM((HEADS, 16, TOK, 2 * D), BF),
            pltpu.VMEM((HEADS, 16, TOK, 2 * D), BF),
            pltpu.VMEM((HEADS, PEERS, TOK, 2 * D), BF),
            pltpu.VMEM((HEADS, PEERS, TOK, 2 * D), BF),
            pltpu.VMEM((HEADS, PEERS, TOK, 2 * D), BF),
            pltpu.VMEM((HEADS, 16, TOK, 2 * D), BF),
            pltpu.VMEM((16, TOK, WROWS), BF),
            pltpu.VMEM((16, TOK, WROWS), BF),
            pltpu.VMEM((HEADS, NX, WPART, 2 * D), BF),
            pltpu.VMEM((HEADS, NX, WPART, 2 * D), BF),
            pltpu.VMEM((HEADS, WPART, 2 * D), BF),
            pltpu.VMEM((HEADS, WPART, 2 * D), BF),
            pltpu.VMEM((HEADS, NX, WPART, 2 * D), BF),
            pltpu.VMEM((ROWS, KEYS), BF),
            pltpu.VMEM((ROWS, KEYS), BF),
            pltpu.VMEM((ROWS, KEYS), BF),
            pltpu.VMEM((ROWS, KEYS), BF),
            pltpu.VMEM((2, ROWS, 2 * D), BF),
            pltpu.VMEM((ROWS, D), F32),
            pltpu.VMEM((ROWS, D), F32),
            pltpu.VMEM((TOK, WIDTH), F32),
            dma((4,)),
            dma((HEADS, 2)),
            *pairs(HEADS, PEERS),
            *pairs(HEADS),
            *pairs(HEADS),
            *pairs(HEADS, PEERS),
            *pairs(HEADS, PEERS),
            *pairs(HEADS),
            *pairs(16),
            *pairs(HEADS, NX),
            *pairs(HEADS),
            *pairs(HEADS, NX),
        ],
        compiler_params=pltpu.CompilerParams(
            collective_id=0, has_side_effects=True, vmem_limit_bytes=62 << 20
        ),
    )(prompt_x, key_value_weight, queries, resp_kv, out_grad, lengths, token_mask)


def solution(mesh):
    rows = P(("grp", "rsp"), None)
    return jax.shard_map(
        local,
        mesh=mesh,
        in_specs=(rows, P(), rows, rows, rows, P(("grp", "rsp")), rows),
        out_specs=(rows, rows, rows, P("rsp", None)),
        check_vma=False,
    )
```

profile of v0, /device:TPU:0, one launch (start us, length us, event | category | flops | bytes accessed | tf_op | source)
XLA Modules:
  0.0 115.3 jit_solution(2794013757562548726)
XLA Ops:
  0.6 108.7 %shard_map.102 = (bf16[256,4096]{1,0:T(8,128)(2,1)}, bf16[256,1024]{1,0:T(8,128)(2,1)}, bf16[64,5120]{1,0:T(8,128)(2,1)}, f32[320,1024]{1,0:T(8,128)}) custom-call(bf16[64,5120]{1,0:T(8,128)(2,1)} %x_hbm.1, bf16[5120,1024]{1,0:T(8,128)(2,1)} %w_hbm.1, bf16[256,4096]{1,0:T(8,128)(2,1)} %q_hbm.1, bf16[256,1024]{1,0:T(8,128)(2,1)} %kv_hbm.1, ...), custom_call_target="tpu_custom_call" | custom-call | tf_op jit(solution)/shard_map/pallas_call | solution.py:383
  109.3 0.0 copy-start.2
  109.3 0.0 copy-start.1
  109.4 3.2 %copy.15 = bf16[256,4096]{1,0:T(8,128)(2,1)} copy(bf16[256,4096]{1,0:T(8,128)(2,1)} %get-tuple-element.8) | data formatting | bytes 4194304
  112.6 0.0 copy-done.2
  112.6 0.0 copy-start
  112.6 0.8 copy.16
  113.4 0.0 copy-done.1
  113.4 0.8 copy.17
  114.2 0.0 copy-done
  114.2 1.1 copy.18
Async XLA Ops:
  109.3 3.2 %copy-start.2 = (bf16[256,1024]{1,0:T(8,128)(2,1)S(1)}, bf16[256,1024]{1,0:T(8,128)(2,1)}, u32[]{:S(2)}) copy-start(bf16[256,1024]{1,0:T(8,128)(2,1)} %get-tuple-element.9) | copy-start | bytes 1572868
  109.3 4.0 %copy-start.1 = (bf16[64,5120]{1,0:T(8,128)(2,1)S(1)}, bf16[64,5120]{1,0:T(8,128)(2,1)}, u32[]{:S(2)}) copy-start(bf16[64,5120]{1,0:T(8,128)(2,1)} %get-tuple-element.10) | copy-start | bytes 1966084
  112.6 1.6 %copy-start = (f32[320,1024]{1,0:T(8,128)S(1)}, f32[320,1024]{1,0:T(8,128)}, u32[]{:S(2)}) copy-start(f32[320,1024]{1,0:T(8,128)} %get-tuple-element.11) | copy-start | bytes 3932164
where the time goes:
time: 115 us
  Pallas kernels  109 us (95%)
  local copies, waits for them, and re-layouts  5.92 us (5%)
    pallas_call x1, Pallas kernels, local(): pl.pallas_call(kernel, out_shape=(jax.ShapeDtypeStruct((2 * SEQ, HEADS *...  109 us
    unnamed x10, local copies, waits for them, and re-layouts  5.92 us

commit v1 on v0

v1 whole, which is shorter than its diff:
```python
import functools

import jax
import jax.numpy as jnp
from jax import lax
from jax.experimental import pallas as pl
from jax.experimental.pallas import tpu as pltpu
from jax.sharding import PartitionSpec as P

HEADS = 4
PER = 8
D = 128
SEQ = 128
ROWS = PER * SEQ
PROMPT = 1024
KEYS = PROMPT + SEQ
TOK = 64
WIDTH = 5120
PEERS = 8
WROWS = 320
GRPS = 8
WPART = 80
KEPT = 2
BF = jnp.bfloat16
F32 = jnp.float32
SCALE = D**-0.5
LOG2E = 1.4426950408889634
MESH = pl.DeviceIdType.MESH
NN = ((1,), (0,))
NT = ((1,), (1,))
TN = ((0,), (0,))


def dot(a, b, dims):
    return lax.dot_general(a, b, (dims, ((), ())), preferred_element_type=F32)


def lanes(start, size=D):
    return pl.ds(pl.multiple_of(start, D), size)


def kernel(
    x_hbm, w_hbm, q_hbm, kv_hbm, d_hbm, len_ref, mask_ref,
    qg_hbm, own_hbm, xg_hbm, wa_hbm,
    x, w, q, d, own, qg, own_g, xg,
    kv, pb, pr, rsr, ga, xr, wf, wp, ws, wr, wa,
    es, ss, rr, qd, xacc,
    in_sem, w_sem, qg_sem, out_sem,
    kv_s, kv_r, kvp_s, kvp_r, p_s, p_r, rs_s, rs_r, ga_s, ga_r,
    x_s, x_r, wp_s, wp_r, w_s, w_r, wa_s, wa_r,
):
    g, r = lax.axis_index("grp"), lax.axis_index("rsp")
    core, at = r % 2, r // 2
    mate = at * 2 + 1 - core
    mine = core * PEERS + at

    def remote(src, dst, send, recv, grp, rsp):
        return pltpu.make_async_remote_copy(
            src_ref=src, dst_ref=dst, send_sem=send, recv_sem=recv,
            device_id=(grp, rsp), device_id_type=MESH,
        )

    def each(count, f):
        def body(j, c):
            f(j)
            return c

        lax.fori_loop(1, count, body, 0)

    loads = [
        pltpu.make_async_copy(src, dst, in_sem.at[n])
        for n, (src, dst) in enumerate(((x_hbm, x), (q_hbm, q), (d_hbm, d), (kv_hbm, own)))
    ]

    def w_loads(h):
        return [
            pltpu.make_async_copy(
                w_hbm.at[:, pl.ds(t * 512 + h * D, D)], w.at[h, :, pl.ds(t * D, D)], w_sem.at[h, t]
            )
            for t in range(2)
        ]

    barrier = pltpu.get_barrier_semaphore()
    each(16, lambda j: pl.semaphore_signal(
        barrier, inc=1, device_id=(g, (r + j) % 16), device_id_type=MESH))
    each(GRPS, lambda j: pl.semaphore_signal(
        barrier, inc=1, device_id=((g + j) % GRPS, r), device_id_type=MESH))

    loads[0].start()
    for h in range(HEADS):
        for c in w_loads(h):
            c.start()
        if h == 1:
            for c in loads[1:]:
                c.start()

    def kv_copy(h, j, there):
        to = (at + j) % PEERS
        slot = core * PEERS + (to if there else at)
        return remote(kv.at[h, slot], kv.at[h, slot], kv_s.at[h, j],
                      kv_r.at[h, to if there else at], g, to * 2 + core)

    def kv_mate(h, side):
        half = kv.at[h, pl.ds(side * PEERS, PEERS)]
        return remote(half, half, kvp_s.at[h], kvp_r.at[h], g, mate)

    def p_copy(h):
        return remote(pb.at[h, pl.ds((1 - core) * PEERS, PEERS)], pr.at[h], p_s.at[h], p_r.at[h], g, mate)

    def rs_copy(h, j, there):
        to = (at + j) % PEERS
        slot = to if there else at
        return remote(pb.at[h, core * PEERS + to], rsr.at[h, slot], rs_s.at[h, j], rs_r.at[h, slot],
                      g, to * 2 + core)

    def ga_copy(h, j, there):
        to = (at + j) % PEERS
        slot = to if there else at
        return remote(ga.at[h, slot], ga.at[h, slot], ga_s.at[h, j], ga_r.at[h, slot], g, to * 2 + core)

    def x_cols(place):
        return lanes(place * 2 * WROWS, 2 * WROWS)

    def x_copy(j, there):
        to = (at + j) % PEERS
        slot = to if there else at
        return remote(x.at[:, x_cols(to)], xr.at[slot], x_s.at[j], x_r.at[slot], g, to * 2 + core)

    def wp_copy(h):
        return remote(wf.at[h, 1 - core], wp.at[h], wp_s.at[h], wp_r.at[h], g, mate)

    def w_copy(h, j, there):
        to = (g + j) % GRPS
        slot = to if there else g
        return remote(ws.at[h, to], wr.at[h, slot], w_s.at[h, j], w_r.at[h, slot], to, r)

    def wa_copy(h, j, there):
        to = (g + j) % GRPS
        slot = to if there else g
        return remote(wa.at[h, slot], wa.at[h, slot], wa_s.at[h, j], wa_r.at[h, slot], to, r)

    def kv_send(h):
        each(PEERS, lambda j: kv_copy(h, j, False).start())

    def kv_relay(h):
        each(PEERS, lambda j: kv_copy(h, j, True).wait_recv())
        kv_mate(h, core).start()

    loads[0].wait()
    for h in range(HEADS):
        for c in w_loads(h):
            c.wait()
        kv[h, mine] = dot(x[...], w[h], NN).astype(BF)
        if h == 0:
            pl.semaphore_wait(barrier, 15 + GRPS - 1)
            kv_send(0)

    for c in loads[1:]:
        c.wait()
    row = lax.broadcasted_iota(jnp.int32, (SEQ, D), 0)
    for n in range(2):
        live = jnp.broadcast_to(mask_ref[n:n + 1, :].astype(F32), (SEQ, SEQ)).T
        live = (live == 1.0) & (row < len_ref[n])
        rows = slice(n * SEQ, (n + 1) * SEQ)

        def clear(c, _, rows=rows, live=live):
            cols = lanes(c * D)
            d[rows, cols] = jnp.where(live, d[rows, cols].astype(F32), 0.0).astype(BF)
            return _

        lax.fori_loop(0, HEADS * PER, clear, 0)
    xr[at] = x[:, x_cols(at)]
    xacc[...] = jnp.zeros_like(xacc)

    kv_relay(0)
    kv_send(1)

    causal = (lax.broadcasted_iota(jnp.int32, (ROWS, SEQ), 1)
              <= lax.broadcasted_iota(jnp.int32, (ROWS, SEQ), 0) % SEQ)

    def own_kv(h, n):
        rows = slice(n * SEQ, (n + 1) * SEQ)
        return own[rows, lanes(h * D)], own[rows, lanes(512 + h * D)]

    def kept(h, n):
        return (h % KEPT) * 2 + n

    def softmax_part(h, n):
        rows = slice(n * SEQ, (n + 1) * SEQ)
        qn = jnp.concatenate([q[rows, lanes((h * PER + t) * D)] for t in range(PER)], 0)
        dn = jnp.concatenate([d[rows, lanes((h * PER + t) * D)] for t in range(PER)], 0)
        keys = kv[h, :, :, 0:D].reshape(PROMPT, D)
        values = kv[h, :, :, D:].reshape(PROMPT, D)
        ko, vo = own_kv(h, n)
        none = jnp.zeros_like(ko)
        both = jnp.concatenate(
            [jnp.concatenate([ko, none], 1), jnp.concatenate([none, vo], 1)], 0)
        last = dot(jnp.concatenate([qn, dn], 1), both, NT)
        scores = jnp.concatenate(
            [dot(qn, keys, NT), jnp.where(causal, last[:, :SEQ], -1e30)], 1)
        pgrad = jnp.concatenate([dot(dn, values, NT), last[:, SEQ:]], 1)
        top = jnp.max(scores, axis=1, keepdims=True)
        e = jnp.exp2((scores - top) * (SCALE * LOG2E))
        inv = 1.0 / jnp.sum(e, axis=1, keepdims=True)
        center = jnp.sum(e * pgrad, axis=1, keepdims=True) * inv
        es[n] = e.astype(BF)
        ss[kept(h, n)] = (e * (pgrad - center)).astype(BF)
        rr[kept(h, n)] = jnp.broadcast_to(inv, (ROWS, D))
        qd[n, :, 0:D] = (qn * inv).astype(BF)
        qd[n, :, D:] = (dn * inv).astype(BF)

    def key_part(h):
        total = []
        for n in range(2):
            dk = dot(qd[n, :, 0:D], ss[kept(h, n)], TN) * SCALE
            dv = dot(qd[n, :, D:], es[n], TN)
            rows = slice(n * SEQ, (n + 1) * SEQ)
            own_g[rows, lanes(h * D)] = dk[:, PROMPT:].astype(BF).T
            own_g[rows, lanes(512 + h * D)] = dv[:, PROMPT:].astype(BF).T
            total.append((dk[:, :PROMPT], dv[:, :PROMPT]))
        dk, dv = total[0][0] + total[1][0], total[0][1] + total[1][1]
        pb[h, :, :, 0:D] = dk.astype(BF).T.reshape(16, TOK, D)
        pb[h, :, :, D:] = dv.astype(BF).T.reshape(16, TOK, D)

    def qg_out(h, n):
        part = (pl.ds(n * SEQ, SEQ), lanes(h * PER * D, PER * D))
        return pltpu.make_async_copy(qg.at[part], qg_hbm.at[part], qg_sem.at[h, n])

    def query_part(h, n):
        rows = slice(n * SEQ, (n + 1) * SEQ)
        keys = jnp.concatenate([kv[h, :, :, 0:D].reshape(PROMPT, D), own_kv(h, n)[0]], 0)
        out = (dot(ss[kept(h, n)], keys, NN) * (rr[kept(h, n)] * SCALE)).astype(BF)
        for t in range(PER):
            qg[rows, lanes((h * PER + t) * D)] = out[t * SEQ:(t + 1) * SEQ]
        qg_out(h, n).start()

    def pair_sum(h):
        p_copy(h).wait_recv()
        half = pb[h, pl.ds(core * PEERS, PEERS)].astype(F32) + pr[h].astype(F32)
        pb[h, pl.ds(core * PEERS, PEERS)] = half.astype(BF)
        each(PEERS, lambda j: rs_copy(h, j, False).start())
        rsr[h, at] = pb[h, mine]

    def group_sum(h):
        each(PEERS, lambda j: rs_copy(h, j, True).wait_recv())
        total = rsr[h, 0].astype(F32)
        for j in range(1, PEERS):
            total += rsr[h, j].astype(F32)
        ga[h, at] = total.astype(BF)
        each(PEERS, lambda j: ga_copy(h, j, False).start())

    def x_part(h):
        def tile(c, _):
            rows = pl.ds(c * 1024, 1024)
            xacc[:, lanes(c * 1024, 1024)] += dot(ga[h, at], w[h, rows, :], NT)
            return _

        lax.fori_loop(0, WIDTH // 1024, tile, 0)

    def w_part(h):
        each(PEERS, lambda j: ga_copy(h, j, True).wait_recv())
        part = dot(xr[...].reshape(PEERS * TOK, 2 * WROWS), ga[h].reshape(PEERS * TOK, 2 * D), TN)
        wf[h] = part.reshape(2, WROWS, 2 * D)
        wp_copy(h).start()

    def w_pair(h):
        wp_copy(h).wait_recv()
        part = (wf[h, core] + wp[h]).astype(BF)
        for i in range(4):
            for t in range(2):
                ws[h, i * 2 + t] = part[i * WPART:(i + 1) * WPART, t * D:(t + 1) * D]
        each(GRPS, lambda j: w_copy(h, j, False).start())
        wr[h, g] = ws[h, g]

    def w_sum(h):
        each(GRPS, lambda j: w_copy(h, j, True).wait_recv())
        total = wr[h, 0].astype(F32)
        for j in range(1, GRPS):
            total += wr[h, j].astype(F32)
        wa[h, g] = total.astype(BF)
        each(GRPS, lambda j: wa_copy(h, j, False).start())

    def wa_out(h):
        return pltpu.make_async_copy(wa.at[h], wa_hbm.at[h], out_sem.at[2 + h])

    def w_out(h):
        each(GRPS, lambda j: wa_copy(h, j, True).wait_recv())
        wa_out(h).start()

    def head(h, c):
        @pl.when(h >= 1)
        def _():
            kv_mate(h, 1 - core).wait_recv()

        @pl.when(h == 0)
        def _():
            kv_mate(0, 1 - core).wait_recv()

        softmax_part(h, 0)

        @pl.when(h >= 1)
        def _():
            pair_sum(h - 1)

        @pl.when(h < HEADS - 2)
        def _():
            kv_send(h + 2)

        softmax_part(h, 1)

        @pl.when(h < HEADS - 1)
        def _():
            kv_relay(h + 1)

        @pl.when(h >= 2)
        def _():
            group_sum(h - 2)

        key_part(h)
        p_copy(h).start()

        @pl.when(h == 0)
        def _():
            each(PEERS, lambda j: x_copy(j, False).start())

        @pl.when(h < HEADS - KEPT)
        def _():
            query_part(h, 0)
            query_part(h, 1)

        return c

    lax.fori_loop(0, HEADS, head, 0)

    own_out = pltpu.make_async_copy(own_g, own_hbm, out_sem.at[0])
    xg_out = pltpu.make_async_copy(xg, xg_hbm, out_sem.at[1])
    own_out.start()
    query_part(2, 0)
    pair_sum(3)
    group_sum(2)
    each(PEERS, lambda j: x_copy(j, True).wait_recv())
    w_part(0)
    query_part(2, 1)
    w_pair(0)
    w_part(1)
    x_part(0)
    w_pair(1)
    x_part(1)
    group_sum(3)
    x_part(2)
    w_sum(0)
    w_part(2)
    query_part(3, 0)
    w_pair(2)
    w_sum(1)
    query_part(3, 1)
    w_part(3)
    x_part(3)
    xg[...] = xacc[...].astype(BF)
    xg_out.start()
    w_pair(3)
    w_sum(2)
    w_out(0)
    w_out(1)
    w_sum(3)
    w_out(2)

    def sent(h, c):
        each(PEERS, lambda j: kv_copy(h, j, False).wait_send())
        kv_mate(h, core).wait_send()
        p_copy(h).wait_send()
        each(PEERS, lambda j: rs_copy(h, j, False).wait_send())
        each(PEERS, lambda j: ga_copy(h, j, False).wait_send())
        wp_copy(h).wait_send()
        each(GRPS, lambda j: w_copy(h, j, False).wait_send())
        for n in range(2):
            qg_out(h, n).wait()
        return c

    lax.fori_loop(0, HEADS, sent, 0)
    each(PEERS, lambda j: x_copy(j, False).wait_send())
    own_out.wait()
    xg_out.wait()
    w_out(3)

    def gathered(h, c):
        each(GRPS, lambda j: wa_copy(h, j, False).wait_send())
        return c

    lax.fori_loop(0, HEADS, gathered, 0)
    for h in range(HEADS):
        wa_out(h).wait()


def finish(qg_in, own_in, xg_in, wa, qg, own_g, xg, wg, sem):
    copies = [
        pltpu.make_async_copy(src, dst, sem.at[n])
        for n, (src, dst) in enumerate(((qg_in, qg), (own_in, own_g), (xg_in, xg)))
    ]
    for c in copies:
        c.start()
    for h in range(HEADS):
        for i in range(4):
            for t in range(2):
                wg[i * WPART:(i + 1) * WPART, t * 512 + h * D:t * 512 + (h + 1) * D] = (
                    wa[h, i * 2 + t].astype(F32))
    for c in copies:
        c.wait()


def local(prompt_x, key_value_weight, queries, resp_kv, out_grad, lengths, token_mask):
    dma = pltpu.SemaphoreType.DMA
    vmem = pl.BlockSpec(memory_space=pltpu.VMEM)
    hbm = pl.BlockSpec(memory_space=pl.ANY)
    pairs = lambda *shape: [dma(shape), dma(shape)]
    qg_shape = jax.ShapeDtypeStruct((2 * SEQ, HEADS * PER * D), BF)
    own_shape = jax.ShapeDtypeStruct((2 * SEQ, 2 * HEADS * D), BF)
    xg_shape = jax.ShapeDtypeStruct((TOK, WIDTH), BF)
    parts = pl.pallas_call(
        kernel,
        out_shape=(
            qg_shape, own_shape, xg_shape,
            jax.ShapeDtypeStruct((HEADS, GRPS, WPART, D), BF),
        ),
        in_specs=[hbm] * 5 + [pl.BlockSpec(memory_space=pltpu.SMEM), vmem],
        out_specs=(hbm,) * 4,
        scratch_shapes=[
            pltpu.VMEM((TOK, WIDTH), BF),
            pltpu.VMEM((HEADS, WIDTH, 2 * D), BF),
            pltpu.VMEM((2 * SEQ, HEADS * PER * D), BF),
            pltpu.VMEM((2 * SEQ, HEADS * PER * D), BF),
            pltpu.VMEM((2 * SEQ, 2 * HEADS * D), BF),
            pltpu.VMEM((2 * SEQ, HEADS * PER * D), BF),
            pltpu.VMEM((2 * SEQ, 2 * HEADS * D), BF),
            pltpu.VMEM((TOK, WIDTH), BF),
            pltpu.VMEM((HEADS, 16, TOK, 2 * D), BF),
            pltpu.VMEM((HEADS, 16, TOK, 2 * D), BF),
            pltpu.VMEM((HEADS, PEERS, TOK, 2 * D), BF),
            pltpu.VMEM((HEADS, PEERS, TOK, 2 * D), BF),
            pltpu.VMEM((HEADS, PEERS, TOK, 2 * D), BF),
            pltpu.VMEM((PEERS, TOK, 2 * WROWS), BF),
            pltpu.VMEM((HEADS, 2, WROWS, 2 * D), F32),
            pltpu.VMEM((HEADS, WROWS, 2 * D), F32),
            pltpu.VMEM((HEADS, GRPS, WPART, D), BF),
            pltpu.VMEM((HEADS, GRPS, WPART, D), BF),
            pltpu.VMEM((HEADS, GRPS, WPART, D), BF),
            pltpu.VMEM((2, ROWS, KEYS), BF),
            pltpu.VMEM((2 * KEPT, ROWS, KEYS), BF),
            pltpu.VMEM((2 * KEPT, ROWS, D), F32),
            pltpu.VMEM((2, ROWS, 2 * D), BF),
            pltpu.VMEM((TOK, WIDTH), F32),
            dma((4,)),
            dma((HEADS, 2)),
            dma((HEADS, 2)),
            dma((2 + HEADS,)),
            *pairs(HEADS, PEERS),
            *pairs(HEADS),
            *pairs(HEADS),
            *pairs(HEADS, PEERS),
            *pairs(HEADS, PEERS),
            *pairs(PEERS),
            *pairs(HEADS),
            *pairs(HEADS, GRPS),
            *pairs(HEADS, GRPS),
        ],
        compiler_params=pltpu.CompilerParams(
            collective_id=0, has_side_effects=True, vmem_limit_bytes=63 << 20
        ),
    )(prompt_x, key_value_weight, queries, resp_kv, out_grad, lengths, token_mask)
    return pl.pallas_call(
        finish,
        out_shape=(
            qg_shape, own_shape, xg_shape,
            jax.ShapeDtypeStruct((WROWS, 2 * HEADS * D), F32),
        ),
        in_specs=[hbm] * 3 + [vmem],
        out_specs=(hbm,) * 3 + (vmem,),
        scratch_shapes=[dma((3,))],
    )(*parts)


def solution(mesh):
    rows = P(("grp", "rsp"), None)
    return jax.shard_map(
        local,
        mesh=mesh,
        in_specs=(rows, P(), rows, rows, rows, P(("grp", "rsp")), rows),
        out_specs=(rows, rows, rows, P("rsp", None)),
        check_vma=False,
    )
```

time: 115 us -> 189 us (1.64)
  Pallas kernels: 109 us -> 188 us
  local copies, waits for them, and re-layouts: 5.92 us -> 0 us
    pallas_call x1 -> x2, Pallas kernels: 109 us -> 188 us  [the longest x1 103 us: local(): pl.pallas_call(finish, out_shape=(qg_shape, own_shape, xg_shape, jax.Shap...]
    unnamed x10 -> x0, local copies, waits for them, and re-layouts: 5.92 us -> none
where the time goes in v1:
time: 189 us
  Pallas kernels  188 us (99%)
    pallas_call x1, Pallas kernels, local(): pl.pallas_call(finish, out_shape=(qg_shape, own_shape, xg_shape, jax.Shap...  103 us
    pallas_call x1, Pallas kernels, local(): pl.pallas_call(kernel, out_shape=(qg_shape, own_shape, xg_shape, jax.Shap...  85.2 us

profile of v1, /device:TPU:0, one launch (start us, length us, event | category | flops | bytes accessed | tf_op | source)
XLA Modules:
  0.0 188.5 jit_solution(9517347174407556730)
XLA Ops:
  0.6 85.2 %shard_map.102 = (bf16[256,4096]{1,0:T(8,128)(2,1)}, bf16[256,1024]{1,0:T(8,128)(2,1)}, bf16[64,5120]{1,0:T(8,128)(2,1)}, bf16[4,8,80,128]{3,2,1,0:T(8,128)(2,1)}) custom-call(bf16[64,5120]{1,0:T(8,128)(2,1)} %x_hbm.1, bf16[5120,1024]{1,0:T(8,128)(2,1)} %w_hbm.1, bf16[256,4096]{1,0:T(8,128)(2,1)} %q_hbm.1, bf16[256,1024]{1,0:T(8,128)(2,1)} %kv_hbm.1, ...), custom_call_target="tpu_custom_call" | custom-call | tf_op jit(solution)/shard_map/pallas_call | solution.py:419
  85.8 102.5 %shard_map.103 = (bf16[256,4096]{1,0:T(8,128)(2,1)}, bf16[256,1024]{1,0:T(8,128)(2,1)}, bf16[64,5120]{1,0:T(8,128)(2,1)}, f32[320,1024]{1,0:T(8,128)}) custom-call(bf16[256,4096]{1,0:T(8,128)(2,1)} %get-tuple-element.8.qg_in, bf16[256,1024]{1,0:T(8,128)(2,1)} %get-tuple-element.9.own_in, bf16[64,5120]{1,0:T(8,128)(2,1)} %get-tuple-element.10.xg_in, ...), custom_call_target="tpu_custom_call" | custom-call | tf_op jit(solution)/shard_map/pallas_call | solution.py:470

commit v2 on v1

v2 whole, which is shorter than its diff:
```python
import functools

import jax
import jax.numpy as jnp
from jax import lax
from jax.experimental import pallas as pl
from jax.experimental.pallas import tpu as pltpu
from jax.sharding import PartitionSpec as P

HEADS = 4
PER = 8
D = 128
SEQ = 128
ROWS = PER * SEQ
PROMPT = 1024
KEYS = PROMPT + SEQ
TOK = 64
WIDTH = 5120
PEERS = 8
WROWS = 320
GRPS = 8
NX = 4
WPART = WROWS // NX
KEPT = 4
BF = jnp.bfloat16
F32 = jnp.float32
SCALE = D**-0.5
LOG2E = 1.4426950408889634
MESH = pl.DeviceIdType.MESH
NN = ((1,), (0,))
NT = ((1,), (1,))
TN = ((0,), (0,))


def dot(a, b, dims):
    return lax.dot_general(a, b, (dims, ((), ())), preferred_element_type=F32)


def lanes(start, size=D):
    return pl.ds(pl.multiple_of(start, D), size)


def kernel(
    x_hbm, w_hbm, q_hbm, kv_hbm, d_hbm, len_ref, mask_ref,
    qg_hbm, own_hbm, xg_hbm, wa_hbm,
    x, w, q, d, own, own_g,
    kv, pb, pr, rsr, ga, xr, wf, wo, wp, ws, wr, zs, zr, wa, wz,
    es, ss, dd, xacc,
    in_sem, w_sem, qg_sem, out_sem,
    kv_s, kv_r, kvp_s, kvp_r, p_s, p_r, rs_s, rs_r, ga_s, ga_r,
    x_s, x_r, wp_s, wp_r, w_s, w_r, z_s, z_r, wa_s, wa_r, wz_s, wz_r,
):
    g, r = lax.axis_index("grp"), lax.axis_index("rsp")
    core, at = r % 2, r // 2
    mate = at * 2 + 1 - core
    gx, gz = g // 2, g % 2
    z_mate = gx * 2 + 1 - gz
    mine = core * PEERS + at

    places = [(at + j) % PEERS for j in range(PEERS)]
    groups = [(g + j) % GRPS for j in range(GRPS)]
    xs = [(gx + j) % NX for j in range(NX)]

    def remote(src, dst, send, recv, grp, rsp):
        return pltpu.make_async_remote_copy(
            src_ref=src, dst_ref=dst, send_sem=send, recv_sem=recv,
            device_id=(grp, rsp), device_id_type=MESH,
        )

    def each(count, f):
        for j in range(1, count):
            f(j)

    loads = [
        pltpu.make_async_copy(src, dst, in_sem.at[n])
        for n, (src, dst) in enumerate(((x_hbm, x), (q_hbm, q), (d_hbm, d), (kv_hbm, own)))
    ]

    def w_loads(h):
        return [
            pltpu.make_async_copy(
                w_hbm.at[:, pl.ds(t * 512 + h * D, D)], w.at[h, :, pl.ds(t * D, D)], w_sem.at[h, t]
            )
            for t in range(2)
        ]

    barrier = pltpu.get_barrier_semaphore()
    each(16, lambda j: pl.semaphore_signal(
        barrier, inc=1, device_id=(g, (r + j) % 16), device_id_type=MESH))
    each(GRPS, lambda j: pl.semaphore_signal(
        barrier, inc=1, device_id=((g + j) % GRPS, r), device_id_type=MESH))

    loads[0].start()
    for h in range(HEADS):
        for c in w_loads(h):
            c.start()
        if h == 1:
            for c in loads[1:]:
                c.start()

    def kv_copy(h, j):
        slot = kv.at[h, mine]
        return remote(slot, slot, kv_s.at[h], kv_r.at[h], g, places[j] * 2 + core)

    def kv_all(h):
        part = kv.at[h, pl.ds(core * PEERS, PEERS - 1)]
        return remote(part, part, kv_s.at[h], kv_r.at[h], g, mate)

    def kv_mate(h, side):
        half = kv.at[h, pl.ds(side * PEERS, PEERS)]
        return remote(half, half, kvp_s.at[h], kvp_r.at[h], g, mate)

    def p_copy(h):
        return remote(pb.at[h, pl.ds((1 - core) * PEERS, PEERS)], pr.at[h], p_s.at[h], p_r.at[h], g, mate)

    def rs_copy(h, j):
        return remote(pb.at[h, core * PEERS + places[j]], rsr.at[h, at], rs_s.at[h], rs_r.at[h],
                      g, places[j] * 2 + core)

    def rs_all(h):
        return remote(pb.at[h, pl.ds(core * PEERS, PEERS - 1)], rsr.at[h, pl.ds(0, PEERS - 1)],
                      rs_s.at[h], rs_r.at[h], g, mate)

    def ga_copy(h, j):
        return remote(ga.at[h, at], ga.at[h, at], ga_s.at[h], ga_r.at[h], g, places[j] * 2 + core)

    def ga_all(h):
        part = ga.at[h, pl.ds(0, PEERS - 1)]
        return remote(part, part, ga_s.at[h], ga_r.at[h], g, mate)

    def x_cols(place):
        return lanes(place * 2 * WROWS, 2 * WROWS)

    def x_copy(j):
        return remote(x.at[:, x_cols(places[j])], xr.at[at], x_s.at[0], x_r.at[0],
                      g, places[j] * 2 + core)

    def x_all():
        part = xr.at[pl.ds(0, PEERS - 1)]
        return remote(part, part, x_s.at[0], x_r.at[0], g, mate)

    def wp_copy(h):
        return remote(wf.at[h], wp.at[h], wp_s.at[h], wp_r.at[h], g, mate)

    def w_copy(h, j):
        return remote(ws.at[h, xs[j]], wr.at[h, gx], w_s.at[h], w_r.at[h], xs[j] * 2 + gz, r)

    def w_all(h):
        return remote(ws.at[h, pl.ds(0, NX - 1)], wr.at[h, pl.ds(0, NX - 1)], w_s.at[h], w_r.at[h], z_mate, r)

    def z_copy(h):
        return remote(zs.at[h], zr.at[h], z_s.at[h], z_r.at[h], z_mate, r)

    def wa_copy(h, j):
        return remote(wa.at[h, gx], wa.at[h, gx], wa_s.at[h], wa_r.at[h], xs[j] * 2 + gz, r)

    def wa_all(h):
        part = wa.at[h, pl.ds(0, NX - 1)]
        return remote(part, part, wa_s.at[h], wa_r.at[h], z_mate, r)

    def wz_copy(j):
        return remote(wz.at[g], wz.at[g], wz_s.at[0], wz_r.at[0], groups[j], r)

    def wz_all():
        part = wz.at[pl.ds(0, GRPS - 1)]
        return remote(part, part, wz_s.at[0], wz_r.at[0], z_mate, r)

    def kv_send(h):
        each(PEERS, lambda j: kv_copy(h, j).start())

    def kv_relay(h):
        kv_all(h).wait_recv()
        kv_mate(h, core).start()

    def project(h):
        for c in w_loads(h):
            c.wait()
        kv[h, mine] = dot(x[...], w[h], NN).astype(BF)

    loads[0].wait()
    project(0)
    pl.semaphore_wait(barrier, 15 + GRPS - 1)
    kv_send(0)
    project(1)

    for c in loads[1:]:
        c.wait()
    row = lax.broadcasted_iota(jnp.int32, (SEQ, D), 0)
    for n in range(2):
        live = jnp.broadcast_to(mask_ref[n:n + 1, :].astype(F32), (SEQ, SEQ)).T
        live = (live == 1.0) & (row < len_ref[n])
        rows = slice(n * SEQ, (n + 1) * SEQ)

        def clear(c, _, rows=rows, live=live):
            cols = lanes(c * D)
            d[rows, cols] = jnp.where(live, d[rows, cols].astype(F32), 0.0).astype(BF)
            return _

        lax.fori_loop(0, HEADS * PER, clear, 0)
    xr[at] = x[:, x_cols(at)]
    xacc[...] = jnp.zeros_like(xacc)

    kv_relay(0)
    kv_send(1)
    project(2)
    project(3)

    causal = (lax.broadcasted_iota(jnp.int32, (ROWS, SEQ), 1)
              <= lax.broadcasted_iota(jnp.int32, (ROWS, SEQ), 0) % SEQ)

    def own_kv(h, n):
        rows = slice(n * SEQ, (n + 1) * SEQ)
        return own[rows, lanes(h * D)], own[rows, lanes(512 + h * D)]

    def kept(h, n):
        return (h % KEPT) * 2 + n

    def softmax_part(h, n):
        rows = slice(n * SEQ, (n + 1) * SEQ)
        qn = jnp.concatenate([q[rows, lanes((h * PER + t) * D)] for t in range(PER)], 0)
        dn = jnp.concatenate([d[rows, lanes((h * PER + t) * D)] for t in range(PER)], 0)
        keys = kv[h, :, :, 0:D].reshape(PROMPT, D)
        values = kv[h, :, :, D:].reshape(PROMPT, D)
        ko, vo = own_kv(h, n)
        none = jnp.zeros_like(ko)
        both = jnp.concatenate(
            [jnp.concatenate([ko, none], 1), jnp.concatenate([none, vo], 1)], 0)
        last = dot(jnp.concatenate([qn, dn], 1), both, NT)
        scores = jnp.concatenate(
            [dot(qn, keys, NT), jnp.where(causal, last[:, :SEQ], -1e30)], 1)
        pgrad = jnp.concatenate([dot(dn, values, NT), last[:, SEQ:]], 1)
        top = jnp.max(scores, axis=1, keepdims=True)
        e = jnp.exp2((scores - top) * (SCALE * LOG2E))
        inv = 1.0 / jnp.sum(e, axis=1, keepdims=True)
        center = jnp.sum(e * pgrad, axis=1, keepdims=True) * inv
        es[n] = e.astype(BF)
        ss[kept(h, n)] = (e * ((pgrad - center) * inv)).astype(BF)
        dd[n] = (dn * inv).astype(BF)

    def key_part(h):
        total = []
        for n in range(2):
            rows = slice(n * SEQ, (n + 1) * SEQ)
            qn = jnp.concatenate([q[rows, lanes((h * PER + t) * D)] for t in range(PER)], 0)
            dk = dot(qn, ss[kept(h, n)], TN) * SCALE
            dv = dot(dd[n], es[n], TN)
            own_g[rows, lanes(h * D)] = dk[:, PROMPT:].astype(BF).T
            own_g[rows, lanes(512 + h * D)] = dv[:, PROMPT:].astype(BF).T
            total.append((dk[:, :PROMPT], dv[:, :PROMPT]))
        dk, dv = total[0][0] + total[1][0], total[0][1] + total[1][1]
        pb[h, :, :, 0:D] = dk.astype(BF).T.reshape(16, TOK, D)
        pb[h, :, :, D:] = dv.astype(BF).T.reshape(16, TOK, D)

    def qg_out(h, n):
        part = (pl.ds(n * SEQ, SEQ), lanes(h * PER * D, PER * D))
        return pltpu.make_async_copy(q.at[part], qg_hbm.at[part], qg_sem.at[h, n])

    def query_part(h, n):
        rows = slice(n * SEQ, (n + 1) * SEQ)
        keys = jnp.concatenate([kv[h, :, :, 0:D].reshape(PROMPT, D), own_kv(h, n)[0]], 0)
        out = (dot(ss[kept(h, n)], keys, NN) * SCALE).astype(BF)
        for t in range(PER):
            q[rows, lanes((h * PER + t) * D)] = out[t * SEQ:(t + 1) * SEQ]
        qg_out(h, n).start()

    def pair_sum(h):
        p_copy(h).wait_recv()
        half = pb[h, pl.ds(core * PEERS, PEERS)].astype(F32) + pr[h].astype(F32)
        pb[h, pl.ds(core * PEERS, PEERS)] = half.astype(BF)
        each(PEERS, lambda j: rs_copy(h, j).start())
        rsr[h, at] = pb[h, mine]

    def group_sum(h):
        rs_all(h).wait_recv()
        total = rsr[h, 0].astype(F32)
        for j in range(1, PEERS):
            total += rsr[h, j].astype(F32)
        ga[h, at] = total.astype(BF)
        each(PEERS, lambda j: ga_copy(h, j).start())

    def x_part(h):
        def tile(c, _):
            rows = pl.ds(c * 1024, 1024)
            xacc[:, lanes(c * 1024, 1024)] += dot(ga[h, at], w[h, rows, :], NT)
            return _

        lax.fori_loop(0, WIDTH // 1024, tile, 0)

    def w_part(h):
        ga_all(h).wait_recv()
        part = dot(xr[...].reshape(PEERS * TOK, 2 * WROWS), ga[h].reshape(PEERS * TOK, 2 * D), TN)
        low, high = part[:WROWS], part[WROWS:]
        wf[h] = jnp.where(core == 0, high, low)
        wo[...] = jnp.where(core == 0, low, high)
        wp_copy(h).start()

    def w_pair(h):
        wp_copy(h).wait_recv()
        ws[h] = (wo[...] + wp[h]).astype(BF).reshape(NX, WPART, 2 * D)
        each(NX, lambda j: w_copy(h, j).start())
        wr[h, gx] = ws[h, gx]

    def w_sum(h):
        w_all(h).wait_recv()
        total = wr[h, 0].astype(F32)
        for j in range(1, NX):
            total += wr[h, j].astype(F32)
        zs[h] = total.astype(BF)
        z_copy(h).start()

    def w_sum_last(h):
        w_all(h).wait_recv()
        total = wr[h, 0].astype(F32)
        for j in range(1, NX):
            total += wr[h, j].astype(F32)
        wz[g] = total.astype(BF)
        each(GRPS, lambda j: wz_copy(j).start())

    def w_out_last(h):
        wz_all().wait_recv()
        for i in range(NX):
            wa[h, i] = (wz[2 * i].astype(F32) + wz[2 * i + 1].astype(F32)).astype(BF)
        wa_out(h).start()

    def z_sum(h):
        z_copy(h).wait_recv()
        wa[h, gx] = (zs[h].astype(F32) + zr[h].astype(F32)).astype(BF)
        each(NX, lambda j: wa_copy(h, j).start())

    def wa_out(h):
        return pltpu.make_async_copy(wa.at[h], wa_hbm.at[h], out_sem.at[2 + h])

    def w_out(h):
        wa_all(h).wait_recv()
        wa_out(h).start()

    def when(cond):
        return pl.when(cond) if not isinstance(cond, bool) else (lambda f: f() if cond else None)

    def head(h, c):
        kv_mate(h, 1 - core).wait_recv()
        softmax_part(h, 0)

        @when(h >= 1)
        def _():
            pair_sum(h - 1)

        @when(h < HEADS - 2)
        def _():
            kv_send(h + 2)

        @when(h == HEADS - 1)
        def _():
            w_part(0)

        softmax_part(h, 1)

        @when(h < HEADS - 1)
        def _():
            kv_relay(h + 1)

        @when(h >= 2)
        def _():
            group_sum(h - 2)

        @when(h == HEADS - 1)
        def _():
            w_pair(0)

        key_part(h)
        p_copy(h).start()

        @when(h == 0)
        def _():
            each(PEERS, lambda j: x_copy(j).start())

        @when(h == 2)
        def _():
            x_all().wait_recv()

        @when(h < HEADS - KEPT)
        def _():
            query_part(h, 0)
            query_part(h, 1)

        return c

    lax.fori_loop(0, HEADS, head, 0)

    own_out = pltpu.make_async_copy(own_g, own_hbm, out_sem.at[0])
    xg_out = pltpu.make_async_copy(x, xg_hbm, out_sem.at[1])
    own_out.start()
    query_part(0, 0)
    pair_sum(3)
    group_sum(2)
    query_part(0, 1)
    w_sum(0)
    query_part(1, 0)
    w_part(1)
    query_part(1, 1)
    w_pair(1)
    group_sum(3)
    x_part(0)
    w_part(2)
    z_sum(0)
    query_part(2, 0)
    w_pair(2)
    w_sum(1)
    query_part(2, 1)
    x_part(1)
    w_part(3)
    z_sum(1)
    query_part(3, 0)
    w_pair(3)
    w_sum(2)
    w_out(0)
    query_part(3, 1)
    x_part(2)
    x_part(3)
    w_sum_last(3)
    z_sum(2)
    w_out(1)
    x_all().wait_send()
    x[...] = xacc[...].astype(BF)
    xg_out.start()

    def sent(h, c):
        kv_all(h).wait_send()
        kv_mate(h, core).wait_send()
        p_copy(h).wait_send()
        rs_all(h).wait_send()
        ga_all(h).wait_send()
        wp_copy(h).wait_send()
        w_all(h).wait_send()
        for n in range(2):
            qg_out(h, n).wait()
        return c

    lax.fori_loop(0, HEADS, sent, 0)
    own_out.wait()
    xg_out.wait()
    w_out(2)
    w_out_last(3)

    def gathered(h, c):
        z_copy(h).wait_send()
        wa_all(h).wait_send()
        return c

    lax.fori_loop(0, HEADS - 1, gathered, 0)
    wz_all().wait_send()
    for h in range(HEADS):
        wa_out(h).wait()


CHUNKS = 4


def finish(qg_in, own_in, xg_in, wa_in, qg, own_g, xg, wg, qv, ov, xv, wav, wv, in_sem, out_sem):
    size = 2 * SEQ // CHUNKS
    moves = [(wa_in, wav, None)]
    for i in range(CHUNKS):
        part = pl.ds(i * size, size)
        moves.append((qg_in.at[part], qv.at[part], qg.at[part]))
    moves += [(own_in, ov, own_g), (xg_in, xv, xg)]
    ins = [pltpu.make_async_copy(src, mid, in_sem.at[n]) for n, (src, mid, _) in enumerate(moves)]
    outs = [pltpu.make_async_copy(mid, dst, out_sem.at[n])
            for n, (_, mid, dst) in enumerate(moves) if dst is not None]
    w_out = pltpu.make_async_copy(wv, wg, out_sem.at[0])
    for c in ins:
        c.start()
    ins[0].wait()
    for h in range(HEADS):
        full = wav[h].astype(F32).reshape(WROWS, 2 * D)
        for t in range(2):
            wv[:, t * 512 + h * D:t * 512 + (h + 1) * D] = full[:, t * D:(t + 1) * D]
    w_out.start()
    for c, o in zip(ins[1:], outs):
        c.wait()
        o.start()
    w_out.wait()
    for o in outs:
        o.wait()


def local(prompt_x, key_value_weight, queries, resp_kv, out_grad, lengths, token_mask):
    dma = pltpu.SemaphoreType.DMA
    vmem = pl.BlockSpec(memory_space=pltpu.VMEM)
    hbm = pl.BlockSpec(memory_space=pl.ANY)
    pairs = lambda *shape: [dma(shape), dma(shape)]
    qg_shape = jax.ShapeDtypeStruct((2 * SEQ, HEADS * PER * D), BF)
    own_shape = jax.ShapeDtypeStruct((2 * SEQ, 2 * HEADS * D), BF)
    xg_shape = jax.ShapeDtypeStruct((TOK, WIDTH), BF)
    parts = pl.pallas_call(
        kernel,
        out_shape=(
            qg_shape, own_shape, xg_shape,
            jax.ShapeDtypeStruct((HEADS, NX, WPART, 2 * D), BF),
        ),
        in_specs=[hbm] * 5 + [pl.BlockSpec(memory_space=pltpu.SMEM), vmem],
        out_specs=(hbm,) * 4,
        scratch_shapes=[
            pltpu.VMEM((TOK, WIDTH), BF),
            pltpu.VMEM((HEADS, WIDTH, 2 * D), BF),
            pltpu.VMEM((2 * SEQ, HEADS * PER * D), BF),
            pltpu.VMEM((2 * SEQ, HEADS * PER * D), BF),
            pltpu.VMEM((2 * SEQ, 2 * HEADS * D), BF),
            pltpu.VMEM((2 * SEQ, 2 * HEADS * D), BF),
            pltpu.VMEM((HEADS, 16, TOK, 2 * D), BF),
            pltpu.VMEM((HEADS, 16, TOK, 2 * D), BF),
            pltpu.VMEM((HEADS, PEERS, TOK, 2 * D), BF),
            pltpu.VMEM((HEADS, PEERS, TOK, 2 * D), BF),
            pltpu.VMEM((HEADS, PEERS, TOK, 2 * D), BF),
            pltpu.VMEM((PEERS, TOK, 2 * WROWS), BF),
            pltpu.VMEM((HEADS, WROWS, 2 * D), F32),
            pltpu.VMEM((WROWS, 2 * D), F32),
            pltpu.VMEM((HEADS, WROWS, 2 * D), F32),
            pltpu.VMEM((HEADS, NX, WPART, 2 * D), BF),
            pltpu.VMEM((HEADS, NX, WPART, 2 * D), BF),
            pltpu.VMEM((HEADS, WPART, 2 * D), BF),
            pltpu.VMEM((HEADS, WPART, 2 * D), BF),
            pltpu.VMEM((HEADS, NX, WPART, 2 * D), BF),
            pltpu.VMEM((GRPS, WPART, 2 * D), BF),
            pltpu.VMEM((2, ROWS, KEYS), BF),
            pltpu.VMEM((2 * KEPT, ROWS, KEYS), BF),
            pltpu.VMEM((2, ROWS, D), BF),
            pltpu.VMEM((TOK, WIDTH), F32),
            dma((4,)),
            dma((HEADS, 2)),
            dma((HEADS, 2)),
            dma((2 + HEADS,)),
            *pairs(HEADS),
            *pairs(HEADS),
            *pairs(HEADS),
            *pairs(HEADS),
            *pairs(HEADS),
            *pairs(1),
            *pairs(HEADS),
            *pairs(HEADS),
            *pairs(HEADS),
            *pairs(HEADS),
            *pairs(1),
        ],
        compiler_params=pltpu.CompilerParams(
            collective_id=0, has_side_effects=True, vmem_limit_bytes=64 << 20
        ),
    )(prompt_x, key_value_weight, queries, resp_kv, out_grad, lengths, token_mask)
    return pl.pallas_call(
        finish,
        out_shape=(
            qg_shape, own_shape, xg_shape,
            jax.ShapeDtypeStruct((WROWS, 2 * HEADS * D), F32),
        ),
        in_specs=[hbm] * 4,
        out_specs=(hbm,) * 4,
        scratch_shapes=[
            pltpu.VMEM(qg_shape.shape, BF),
            pltpu.VMEM(own_shape.shape, BF),
            pltpu.VMEM(xg_shape.shape, BF),
            pltpu.VMEM((HEADS, NX, WPART, 2 * D), BF),
            pltpu.VMEM((WROWS, 2 * HEADS * D), F32),
            dma((3 + CHUNKS,)),
            dma((3 + CHUNKS,)),
        ],
        compiler_params=pltpu.CompilerParams(vmem_limit_bytes=60 << 20),
    )(*parts)


def solution(mesh):
    rows = P(("grp", "rsp"), None)
    return jax.shard_map(
        local,
        mesh=mesh,
        in_specs=(rows, P(), rows, rows, rows, P(("grp", "rsp")), rows),
        out_specs=(rows, rows, rows, P("rsp", None)),
        check_vma=False,
    )
```

time: 189 us -> 88.6 us (0.47)
  Pallas kernels: 188 us -> 87 us
    pallas_call x1, Pallas kernels: 103 us -> 3.51 us  [local(): pl.pallas_call(finish, out_shape=(qg_shape, own_shape, xg_shape, jax.Shap...]
where the time goes in v2:
time: 88.6 us; the launch traced here: 87.8 us
  Pallas kernels  87 us (98%)
    pallas_call x1, Pallas kernels, local(): pl.pallas_call(kernel, out_shape=(qg_shape, own_shape, xg_shape, jax.Shap...  83.5 us
    pallas_call x1, Pallas kernels, local(): pl.pallas_call(finish, out_shape=(qg_shape, own_shape, xg_shape, jax.Shap...  3.51 us

profile of v2, /device:TPU:0, one launch (start us, length us, event | category | flops | bytes accessed | tf_op | source)
XLA Modules:
  0.0 87.8 jit_solution(5964081521211574440)
XLA Ops:
  0.6 83.5 %shard_map.102 = (bf16[256,4096]{1,0:T(8,128)(2,1)}, bf16[256,1024]{1,0:T(8,128)(2,1)}, bf16[64,5120]{1,0:T(8,128)(2,1)}, bf16[4,4,80,256]{3,2,1,0:T(8,128)(2,1)}) custom-call(bf16[64,5120]{1,0:T(8,128)(2,1)} %x_hbm.1, bf16[5120,1024]{1,0:T(8,128)(2,1)} %w_hbm.1, bf16[256,4096]{1,0:T(8,128)(2,1)} %q_hbm.1, bf16[256,1024]{1,0:T(8,128)(2,1)} %kv_hbm.1, ...), custom_call_target="tpu_custom_call" | custom-call | tf_op jit(solution)/shard_map/pallas_call | solution.py:494
  84.1 3.5 %shard_map.103 = (bf16[256,4096]{1,0:T(8,128)(2,1)}, bf16[256,1024]{1,0:T(8,128)(2,1)}, bf16[64,5120]{1,0:T(8,128)(2,1)}, f32[320,1024]{1,0:T(8,128)}) custom-call(bf16[256,4096]{1,0:T(8,128)(2,1)} %get-tuple-element.8.qg_in, bf16[256,1024]{1,0:T(8,128)(2,1)} %get-tuple-element.9.own_in, bf16[64,5120]{1,0:T(8,128)(2,1)} %get-tuple-element.10.xg_in, ...), custom_call_target="tpu_custom_call" | custom-call | tf_op jit(solution)/shard_map/pallas_call | solution.py:548

commit v3 on v2

--- a/solution.py
+++ b/solution.py
@@ -19,8 +19,7 @@
 PEERS = 8
 WROWS = 320
 GRPS = 8
-NX = 4
-WPART = WROWS // NX
+WPART = 80
 KEPT = 4
 BF = jnp.bfloat16
 F32 = jnp.float32
@@ -44,22 +43,19 @@
     x_hbm, w_hbm, q_hbm, kv_hbm, d_hbm, len_ref, mask_ref,
     qg_hbm, own_hbm, xg_hbm, wa_hbm,
     x, w, q, d, own, own_g,
-    kv, pb, pr, rsr, ga, xr, wf, wo, wp, ws, wr, zs, zr, wa, wz,
+    kv, pb, pr, rsr, ga, xr, wf, wo, wp, ws, wr, wa,
     es, ss, dd, xacc,
     in_sem, w_sem, qg_sem, out_sem,
     kv_s, kv_r, kvp_s, kvp_r, p_s, p_r, rs_s, rs_r, ga_s, ga_r,
-    x_s, x_r, wp_s, wp_r, w_s, w_r, z_s, z_r, wa_s, wa_r, wz_s, wz_r,
+    x_s, x_r, wp_s, wp_r, w_s, w_r, wa_s, wa_r,
 ):
     g, r = lax.axis_index("grp"), lax.axis_index("rsp")
     core, at = r % 2, r // 2
     mate = at * 2 + 1 - core
-    gx, gz = g // 2, g % 2
-    z_mate = gx * 2 + 1 - gz
     mine = core * PEERS + at
 
     places = [(at + j) % PEERS for j in range(PEERS)]
     groups = [(g + j) % GRPS for j in range(GRPS)]
-    xs = [(gx + j) % NX for j in range(NX)]
 
     def remote(src, dst, send, recv, grp, rsp):
         return pltpu.make_async_remote_copy(
@@ -98,17 +94,17 @@
             for c in loads[1:]:
                 c.start()
 
-    def kv_copy(h, j):
-        slot = kv.at[h, mine]
-        return remote(slot, slot, kv_s.at[h], kv_r.at[h], g, places[j] * 2 + core)
-
-    def kv_all(h):
-        part = kv.at[h, pl.ds(core * PEERS, PEERS - 1)]
-        return remote(part, part, kv_s.at[h], kv_r.at[h], g, mate)
-
-    def kv_mate(h, side):
-        half = kv.at[h, pl.ds(side * PEERS, PEERS)]
-        return remote(half, half, kvp_s.at[h], kvp_r.at[h], g, mate)
+    def kv_copy(h, n, j):
+        part = (pl.ds(h, n), mine)
+        return remote(kv.at[part], kv.at[part], kv_s.at[h], kv_r.at[h], g, places[j] * 2 + core)
+
+    def kv_all(h, n):
+        part = (pl.ds(h, n), pl.ds(core * PEERS, PEERS - 1))
+        return remote(kv.at[part], kv.at[part], kv_s.at[h], kv_r.at[h], g, mate)
+
+    def kv_mate(h, n, side):
+        part = (pl.ds(h, n), pl.ds(side * PEERS, PEERS))
+        return remote(kv.at[part], kv.at[part], kvp_s.at[h], kvp_r.at[h], g, mate)
 
     def p_copy(h):
         return remote(pb.at[h, pl.ds((1 - core) * PEERS, PEERS)], pr.at[h], p_s.at[h], p_r.at[h], g, mate)
@@ -139,38 +135,32 @@
         part = xr.at[pl.ds(0, PEERS - 1)]
         return remote(part, part, x_s.at[0], x_r.at[0], g, mate)
 
-    def wp_copy(h):
-        return remote(wf.at[h], wp.at[h], wp_s.at[h], wp_r.at[h], g, mate)
-
-    def w_copy(h, j):
-        return remote(ws.at[h, xs[j]], wr.at[h, gx], w_s.at[h], w_r.at[h], xs[j] * 2 + gz, r)
-
-    def w_all(h):
-        return remote(ws.at[h, pl.ds(0, NX - 1)], wr.at[h, pl.ds(0, NX - 1)], w_s.at[h], w_r.at[h], z_mate, r)
-
-    def z_copy(h):
-        return remote(zs.at[h], zr.at[h], z_s.at[h], z_r.at[h], z_mate, r)
-
-    def wa_copy(h, j):
-        return remote(wa.at[h, gx], wa.at[h, gx], wa_s.at[h], wa_r.at[h], xs[j] * 2 + gz, r)
-
-    def wa_all(h):
-        part = wa.at[h, pl.ds(0, NX - 1)]
-        return remote(part, part, wa_s.at[h], wa_r.at[h], z_mate, r)
-
-    def wz_copy(j):
-        return remote(wz.at[g], wz.at[g], wz_s.at[0], wz_r.at[0], groups[j], r)
-
-    def wz_all():
-        part = wz.at[pl.ds(0, GRPS - 1)]
-        return remote(part, part, wz_s.at[0], wz_r.at[0], z_mate, r)
-
-    def kv_send(h):
-        each(PEERS, lambda j: kv_copy(h, j).start())
-
-    def kv_relay(h):
-        kv_all(h).wait_recv()
-        kv_mate(h, core).start()
+    def wp_copy(h, n):
+        part = pl.ds(h, n)
+        return remote(wf.at[part], wp.at[part], wp_s.at[h], wp_r.at[h], g, mate)
+
+    def w_copy(h, n, j):
+        part = pl.ds(h, n)
+        return remote(ws.at[part, groups[j]], wr.at[part, g], w_s.at[h], w_r.at[h], groups[j], r)
+
+    def w_all(h, n):
+        part = (pl.ds(h, n), pl.ds(0, GRPS - 1))
+        return remote(ws.at[part], wr.at[part], w_s.at[h], w_r.at[h], groups[1], r)
+
+    def wa_copy(h, n, j):
+        part = (pl.ds(h, n), g)
+        return remote(wa.at[part], wa.at[part], wa_s.at[h], wa_r.at[h], groups[j], r)
+
+    def wa_all(h, n):
+        part = (pl.ds(h, n), pl.ds(0, GRPS - 1))
+        return remote(wa.at[part], wa.at[part], wa_s.at[h], wa_r.at[h], groups[1], r)
+
+    def kv_send(h, n):
+        each(PEERS, lambda j: kv_copy(h, n, j).start())
+
+    def kv_relay(h, n):
+        kv_all(h, n).wait_recv()
+        kv_mate(h, n, core).start()
 
     def project(h):
         for c in w_loads(h):
@@ -180,7 +170,7 @@
     loads[0].wait()
     project(0)
     pl.semaphore_wait(barrier, 15 + GRPS - 1)
-    kv_send(0)
+    kv_send(0, 1)
     project(1)
 
     for c in loads[1:]:
@@ -200,8 +190,8 @@
     xr[at] = x[:, x_cols(at)]
     xacc[...] = jnp.zeros_like(xacc)
 
-    kv_relay(0)
-    kv_send(1)
+    kv_relay(0, 1)
+    kv_send(1, 1)
     project(2)
     project(3)
 
@@ -287,85 +277,80 @@
         lax.fori_loop(0, WIDTH // 1024, tile, 0)
 
     def w_part(h):
-        ga_all(h).wait_recv()
         part = dot(xr[...].reshape(PEERS * TOK, 2 * WROWS), ga[h].reshape(PEERS * TOK, 2 * D), TN)
         low, high = part[:WROWS], part[WROWS:]
-        wf[h] = jnp.where(core == 0, high, low)
-        wo[...] = jnp.where(core == 0, low, high)
-        wp_copy(h).start()
-
-    def w_pair(h):
-        wp_copy(h).wait_recv()
-        ws[h] = (wo[...] + wp[h]).astype(BF).reshape(NX, WPART, 2 * D)
-        each(NX, lambda j: w_copy(h, j).start())
-        wr[h, gx] = ws[h, gx]
-
-    def w_sum(h):
-        w_all(h).wait_recv()
-        total = wr[h, 0].astype(F32)
-        for j in range(1, NX):
-            total += wr[h, j].astype(F32)
-        zs[h] = total.astype(BF)
-        z_copy(h).start()
-
-    def w_sum_last(h):
-        w_all(h).wait_recv()
-        total = wr[h, 0].astype(F32)
-        for j in range(1, NX):
-            total += wr[h, j].astype(F32)
-        wz[g] = total.astype(BF)
-        each(GRPS, lambda j: wz_copy(j).start())
-
-    def w_out_last(h):
-        wz_all().wait_recv()
-        for i in range(NX):
-            wa[h, i] = (wz[2 * i].astype(F32) + wz[2 * i + 1].astype(F32)).astype(BF)
-        wa_out(h).start()
-
-    def z_sum(h):
-        z_copy(h).wait_recv()
-        wa[h, gx] = (zs[h].astype(F32) + zr[h].astype(F32)).astype(BF)
-        each(NX, lambda j: wa_copy(h, j).start())
-
-    def wa_out(h):
-        return pltpu.make_async_copy(wa.at[h], wa_hbm.at[h], out_sem.at[2 + h])
-
-    def w_out(h):
-        wa_all(h).wait_recv()
-        wa_out(h).start()
+        wf[h] = jnp.where(core == 0, high, low).astype(BF)
+        wo[h % 2] = jnp.where(core == 0, low, high)
+
+    def w_send(h, n):
+        for i in range(h, h + n):
+            ga_all(i).wait_recv()
+            w_part(i)
+        wp_copy(h, n).start()
+
+    def w_pair(h, n):
+        wp_copy(h, n).wait_recv()
+        for k in range(h, h + n):
+            part = (wo[k % 2] + wp[k].astype(F32)).astype(BF)
+            for i in range(4):
+                for t in range(2):
+                    ws[k, i * 2 + t] = part[i * WPART:(i + 1) * WPART, t * D:(t + 1) * D]
+        each(GRPS, lambda j: w_copy(h, n, j).start())
+        for k in range(h, h + n):
+            wr[k, g] = ws[k, g]
+
+    def w_sum(h, n):
+        w_all(h, n).wait_recv()
+        for k in range(h, h + n):
+            total = wr[k, 0].astype(F32)
+            for j in range(1, GRPS):
+                total += wr[k, j].astype(F32)
+            wa[k, g] = total.astype(BF)
+        each(GRPS, lambda j: wa_copy(h, n, j).start())
+
+    def wa_out(h, n):
+        part = pl.ds(h, n)
+        return pltpu.make_async_copy(wa.at[part], wa_hbm.at[part], out_sem.at[2 + h])
+
+    def w_out(h, n):
+        wa_all(h, n).wait_recv()
+        wa_out(h, n).start()
 
     def when(cond):
         return pl.when(cond) if not isinstance(cond, bool) else (lambda f: f() if cond else None)
 
     def head(h, c):
-        kv_mate(h, 1 - core).wait_recv()
+        @when(h < 2)
+        def _():
+            kv_mate(h, 1, 1 - core).wait_recv()
+
+        @when(h == 2)
+        def _():
+            kv_mate(2, 2, 1 - core).wait_recv()
+
         softmax_part(h, 0)
 
         @when(h >= 1)
         def _():
             pair_sum(h - 1)
 
-        @when(h < HEADS - 2)
-        def _():
-            kv_send(h + 2)
-
-        @when(h == HEADS - 1)
-        def _():
-            w_part(0)
+        @when(h == 0)
+        def _():
+            kv_send(2, 2)
 
         softmax_part(h, 1)
 
-        @when(h < HEADS - 1)
-        def _():
-            kv_relay(h + 1)
+        @when(h == 0)
+        def _():
+            kv_relay(1, 1)
+
+        @when(h == 1)
+        def _():
+            kv_relay(2, 2)
 
         @when(h >= 2)
         def _():
             group_sum(h - 2)
-
-        @when(h == HEADS - 1)
-        def _():
-            w_pair(0)
 
         key_part(h)
         p_copy(h).start()
@@ -373,15 +358,6 @@
         @when(h == 0)
         def _():
             each(PEERS, lambda j: x_copy(j).start())
-
-        @when(h == 2)
-        def _():
-            x_all().wait_recv()
-
-        @when(h < HEADS - KEPT)
-        def _():
-            query_part(h, 0)
-            query_part(h, 1)
 
         return c
 
@@ -394,63 +370,51 @@
     pair_sum(3)
     group_sum(2)
     query_part(0, 1)
-    w_sum(0)
+    x_all().wait_recv()
+    w_send(0, 2)
     query_part(1, 0)
-    w_part(1)
-    query_part(1, 1)
-    w_pair(1)
+    w_pair(0, 2)
     group_sum(3)
     x_part(0)
-    w_part(2)
-    z_sum(0)
+    query_part(1, 1)
+    w_send(2, 1)
+    x_part(1)
+    w_pair(2, 1)
     query_part(2, 0)
-    w_pair(2)
-    w_sum(1)
     query_part(2, 1)
-    x_part(1)
-    w_part(3)
-    z_sum(1)
+    w_send(3, 1)
+    w_sum(0, 2)
+    x_part(2)
+    w_pair(3, 1)
+    w_sum(2, 1)
     query_part(3, 0)
-    w_pair(3)
-    w_sum(2)
-    w_out(0)
     query_part(3, 1)
-    x_part(2)
     x_part(3)
-    w_sum_last(3)
-    z_sum(2)
-    w_out(1)
     x_all().wait_send()
     x[...] = xacc[...].astype(BF)
     xg_out.start()
-
-    def sent(h, c):
-        kv_all(h).wait_send()
-        kv_mate(h, core).wait_send()
+    w_sum(3, 1)
+    w_out(0, 2)
+
+    for h in range(HEADS):
         p_copy(h).wait_send()
         rs_all(h).wait_send()
         ga_all(h).wait_send()
-        wp_copy(h).wait_send()
-        w_all(h).wait_send()
         for n in range(2):
             qg_out(h, n).wait()
-        return c
-
-    lax.fori_loop(0, HEADS, sent, 0)
+    for h, n in ((0, 1), (1, 1), (2, 2)):
+        kv_all(h, n).wait_send()
+        kv_mate(h, n, core).wait_send()
     own_out.wait()
+    w_out(2, 1)
+    for h, n in ((0, 2), (2, 1), (3, 1)):
+        wp_copy(h, n).wait_send()
+        w_all(h, n).wait_send()
     xg_out.wait()
-    w_out(2)
-    w_out_last(3)
-
-    def gathered(h, c):
-        z_copy(h).wait_send()
-        wa_all(h).wait_send()
-        return c
-
-    lax.fori_loop(0, HEADS - 1, gathered, 0)
-    wz_all().wait_send()
-    for h in range(HEADS):
-        wa_out(h).wait()
+    w_out(3, 1)
+    for h, n in ((0, 2), (2, 1), (3, 1)):
+        wa_all(h, n).wait_send()
+        wa_out(h, n).wait()
 
 
 CHUNKS = 4
@@ -471,9 +435,10 @@
         c.start()
     ins[0].wait()
     for h in range(HEADS):
-        full = wav[h].astype(F32).reshape(WROWS, 2 * D)
-        for t in range(2):
-            wv[:, t * 512 + h * D:t * 512 + (h + 1) * D] = full[:, t * D:(t + 1) * D]
+        for i in range(4):
+            for t in range(2):
+                wv[i * WPART:(i + 1) * WPART, t * 512 + h * D:t * 512 + (h + 1) * D] = (
+                    wav[h, i * 2 + t].astype(F32))
     w_out.start()
     for c, o in zip(ins[1:], outs):
         c.wait()
@@ -495,7 +460,7 @@
         kernel,
         out_shape=(
             qg_shape, own_shape, xg_shape,
-            jax.ShapeDtypeStruct((HEADS, NX, WPART, 2 * D), BF),
+            jax.ShapeDtypeStruct((HEADS, GRPS, WPART, D), BF),
         ),
         in_specs=[hbm] * 5 + [pl.BlockSpec(memory_space=pltpu.SMEM), vmem],
         out_specs=(hbm,) * 4,
@@ -512,15 +477,12 @@
             pltpu.VMEM((HEADS, PEERS, TOK, 2 * D), BF),
             pltpu.VMEM((HEADS, PEERS, TOK, 2 * D), BF),
             pltpu.VMEM((PEERS, TOK, 2 * WROWS), BF),
-            pltpu.VMEM((HEADS, WROWS, 2 * D), F32),
-            pltpu.VMEM((WROWS, 2 * D), F32),
-            pltpu.VMEM((HEADS, WROWS, 2 * D), F32),
-            pltpu.VMEM((HEADS, NX, WPART, 2 * D), BF),
-            pltpu.VMEM((HEADS, NX, WPART, 2 * D), BF),
-            pltpu.VMEM((HEADS, WPART, 2 * D), BF),
-            pltpu.VMEM((HEADS, WPART, 2 * D), BF),
-            pltpu.VMEM((HEADS, NX, WPART, 2 * D), BF),
-            pltpu.VMEM((GRPS, WPART, 2 * D), BF),
+            pltpu.VMEM((HEADS, WROWS, 2 * D), BF),
+            pltpu.VMEM((2, WROWS, 2 * D), F32),
+            pltpu.VMEM((HEADS, WROWS, 2 * D), BF),
+            pltpu.VMEM((HEADS, GRPS, WPART, D), BF),
+            pltpu.VMEM((HEADS, GRPS, WPART, D), BF),
+            pltpu.VMEM((HEADS, GRPS, WPART, D), BF),
             pltpu.VMEM((2, ROWS, KEYS), BF),
             pltpu.VMEM((2 * KEPT, ROWS, KEYS), BF),
             pltpu.VMEM((2, ROWS, D), BF),
@@ -538,8 +500,6 @@
             *pairs(HEADS),
             *pairs(HEADS),
             *pairs(HEADS),
-            *pairs(HEADS),
-            *pairs(1),
         ],
         compiler_params=pltpu.CompilerParams(
             collective_id=0, has_side_effects=True, vmem_limit_bytes=64 << 20
@@ -557,7 +517,7 @@
             pltpu.VMEM(qg_shape.shape, BF),
             pltpu.VMEM(own_shape.shape, BF),
             pltpu.VMEM(xg_shape.shape, BF),
-            pltpu.VMEM((HEADS, NX, WPART, 2 * D), BF),
+            pltpu.VMEM((HEADS, GRPS, WPART, D), BF),
             pltpu.VMEM((WROWS, 2 * HEADS * D), F32),
             dma((3 + CHUNKS,)),
             dma((3 + CHUNKS,)),

time: 88.6 us -> 84.6 us (0.955)
  Pallas kernels: 87 us -> 83.6 us
    pallas_call x1, Pallas kernels: 83.5 us -> 80.1 us  [local(): pl.pallas_call(kernel, out_shape=(qg_shape, own_shape, xg_shape, jax.Shap...]
where the time goes in v3:
time: 84.6 us; the launch traced here: 84.4 us
  Pallas kernels  83.6 us (99%)
    pallas_call x1, Pallas kernels, local(): pl.pallas_call(kernel, out_shape=(qg_shape, own_shape, xg_shape, jax.Shap...  80.1 us
    pallas_call x1, Pallas kernels, local(): pl.pallas_call(finish, out_shape=(qg_shape, own_shape, xg_shape, jax.Shap...  3.51 us

profile of v3, /device:TPU:0, one launch (start us, length us, event | category | flops | bytes accessed | tf_op | source)
XLA Modules:
  0.0 84.4 jit_solution(13910269407493135212)
XLA Ops:
  0.6 80.1 %shard_map.102 = (bf16[256,4096]{1,0:T(8,128)(2,1)}, bf16[256,1024]{1,0:T(8,128)(2,1)}, bf16[64,5120]{1,0:T(8,128)(2,1)}, bf16[4,8,80,128]{3,2,1,0:T(8,128)(2,1)}) custom-call(bf16[64,5120]{1,0:T(8,128)(2,1)} %x_hbm.1, bf16[5120,1024]{1,0:T(8,128)(2,1)} %w_hbm.1, bf16[256,4096]{1,0:T(8,128)(2,1)} %q_hbm.1, bf16[256,1024]{1,0:T(8,128)(2,1)} %kv_hbm.1, ...), custom_call_target="tpu_custom_call" | custom-call | tf_op jit(solution)/shard_map/pallas_call | solution.py:459
  80.8 3.5 %shard_map.103 = (bf16[256,4096]{1,0:T(8,128)(2,1)}, bf16[256,1024]{1,0:T(8,128)(2,1)}, bf16[64,5120]{1,0:T(8,128)(2,1)}, f32[320,1024]{1,0:T(8,128)}) custom-call(bf16[256,4096]{1,0:T(8,128)(2,1)} %get-tuple-element.8.qg_in, bf16[256,1024]{1,0:T(8,128)(2,1)} %get-tuple-element.9.own_in, bf16[64,5120]{1,0:T(8,128)(2,1)} %get-tuple-element.10.xg_in, ...), custom_call_target="tpu_custom_call" | custom-call | tf_op jit(solution)/shard_map/pallas_call | solution.py:508

commit v4 on v3

--- a/solution.py
+++ b/solution.py
@@ -190,9 +190,9 @@
     xr[at] = x[:, x_cols(at)]
     xacc[...] = jnp.zeros_like(xacc)
 
+    project(2)
     kv_relay(0, 1)
     kv_send(1, 1)
-    project(2)
     project(3)
 
     causal = (lax.broadcasted_iota(jnp.int32, (ROWS, SEQ), 1)
@@ -348,9 +348,9 @@
         def _():
             kv_relay(2, 2)
 
-        @when(h >= 2)
-        def _():
-            group_sum(h - 2)
+        @when(h == 2)
+        def _():
+            group_sum(0)
 
         key_part(h)
         p_copy(h).start()
@@ -366,34 +366,35 @@
     own_out = pltpu.make_async_copy(own_g, own_hbm, out_sem.at[0])
     xg_out = pltpu.make_async_copy(x, xg_hbm, out_sem.at[1])
     own_out.start()
-    query_part(0, 0)
+    group_sum(1)
     pair_sum(3)
     group_sum(2)
+    query_part(0, 0)
     query_part(0, 1)
     x_all().wait_recv()
+    x_part(0)
     w_send(0, 2)
     query_part(1, 0)
     w_pair(0, 2)
     group_sum(3)
-    x_part(0)
     query_part(1, 1)
     w_send(2, 1)
     x_part(1)
     w_pair(2, 1)
     query_part(2, 0)
-    query_part(2, 1)
     w_send(3, 1)
     w_sum(0, 2)
+    w_pair(3, 1)
+    query_part(2, 1)
     x_part(2)
-    w_pair(3, 1)
     w_sum(2, 1)
     query_part(3, 0)
+    w_sum(3, 1)
     query_part(3, 1)
     x_part(3)
     x_all().wait_send()
     x[...] = xacc[...].astype(BF)
     xg_out.start()
-    w_sum(3, 1)
     w_out(0, 2)
 
     for h in range(HEADS):
@@ -433,6 +434,9 @@
     w_out = pltpu.make_async_copy(wv, wg, out_sem.at[0])
     for c in ins:
         c.start()
+    for c, o in zip(ins[1:], outs):
+        c.wait()
+        o.start()
     ins[0].wait()
     for h in range(HEADS):
         for i in range(4):
@@ -440,9 +444,6 @@
                 wv[i * WPART:(i + 1) * WPART, t * 512 + h * D:t * 512 + (h + 1) * D] = (
                     wav[h, i * 2 + t].astype(F32))
     w_out.start()
-    for c, o in zip(ins[1:], outs):
-        c.wait()
-        o.start()
     w_out.wait()
     for o in outs:
         o.wait()

time: 84.6 us -> 86.8 us (1.026)
  Pallas kernels: 83.6 us -> 85.9 us
    pallas_call x1, Pallas kernels: 80.1 us -> 82.4 us  [local(): pl.pallas_call(kernel, out_shape=(qg_shape, own_shape, xg_shape, jax.Shap...]
where the time goes in v4:
time: 86.8 us; the launch traced here: 86.7 us
  Pallas kernels  85.9 us (99%)
    pallas_call x1, Pallas kernels, local(): pl.pallas_call(kernel, out_shape=(qg_shape, own_shape, xg_shape, jax.Shap...  82.4 us
    pallas_call x1, Pallas kernels, local(): pl.pallas_call(finish, out_shape=(qg_shape, own_shape, xg_shape, jax.Shap...  3.5 us

profile of v4, /device:TPU:0, one launch (start us, length us, event | category | flops | bytes accessed | tf_op | source)
XLA Modules:
  0.0 86.7 jit_solution(4388039153052925698)
XLA Ops:
  0.6 82.4 %shard_map.102 = (bf16[256,4096]{1,0:T(8,128)(2,1)}, bf16[256,1024]{1,0:T(8,128)(2,1)}, bf16[64,5120]{1,0:T(8,128)(2,1)}, bf16[4,8,80,128]{3,2,1,0:T(8,128)(2,1)}) custom-call(bf16[64,5120]{1,0:T(8,128)(2,1)} %x_hbm.1, bf16[5120,1024]{1,0:T(8,128)(2,1)} %w_hbm.1, bf16[256,4096]{1,0:T(8,128)(2,1)} %q_hbm.1, bf16[256,1024]{1,0:T(8,128)(2,1)} %kv_hbm.1, ...), custom_call_target="tpu_custom_call" | custom-call | tf_op jit(solution)/shard_map/pallas_call | solution.py:460
  83.0 3.5 %shard_map.103 = (bf16[256,4096]{1,0:T(8,128)(2,1)}, bf16[256,1024]{1,0:T(8,128)(2,1)}, bf16[64,5120]{1,0:T(8,128)(2,1)}, f32[320,1024]{1,0:T(8,128)}) custom-call(bf16[256,4096]{1,0:T(8,128)(2,1)} %get-tuple-element.8.qg_in, bf16[256,1024]{1,0:T(8,128)(2,1)} %get-tuple-element.9.own_in, bf16[64,5120]{1,0:T(8,128)(2,1)} %get-tuple-element.10.xg_in, ...), custom_call_target="tpu_custom_call" | custom-call | tf_op jit(solution)/shard_map/pallas_call | solution.py:509
